TPU v7x, 32 devices: a whole 2x2x4 slice. The times are simulated.
32 devices in a mesh: grp: 2 (over y), sta: 4 (over z), hr: 2 (over x), sub: 2 (over core).
Axes of the slice: x: 2, y: 2, z: 4, core: 2. Of those that a mesh axis runs over, the one named last changes fastest.
Arguments:
- spectra: bfloat16 [4, 1000, 2, 4096], P(('grp', 'hr'), 'sub', None, 'sta'), parts along dimension 0, may hold values from -400 to 400
- pair_blocks: int32 [4, 2], replicated, may hold values from 0 to 31, as said below
- pair_owner: int32 [4], replicated, may hold values from 0 to 3, as said below
- block_members: int32 [32, 128], P('sta'), may hold values from 0 to 1023, as said below
Outputs:
- correlations: bfloat16 [32, 12, 128, 128], P(('grp', 'hr', 'sub'), 'sta'), parts along dimension 0
There are 2 independent parts, one for each index of `grp`. A program takes and returns all parts, laid end to end along the dimension named above; an argument that names none is the same for every part. Nothing has to cross between parts.
Inputs may be any that keep to these rules, and one draw needn't show every extreme that they name: `pair_blocks`: each row names two different blocks; block g holds stations of index g // 8 of sta. The blocks of the pairs of owner o lie on indices o, o + 1, o + 2 or o + 3 (mod 4) of sta, and the distinct blocks named by the pairs of one owner lie on distinct indices of sta. `pair_owner`: at most 3 pairs share an owner, and some owner has exactly 3. `block_members`: the 8 rows of the blocks of one index of sta hold each of 0 to 1023 once.
All inputs are finite; a program needn't handle non-finite values.
Results may differ from a plain program's by a relative error of at most 0.0063.
Values may be sent and summed in bfloat16 or wider, within the bound.
No kernel may reach another device: no remote copies, remote signals or barrier semaphores. Data moves between devices by JAX's collectives and lax.ppermute only.
A program may use at most 64 MiB of HBM per device.

v0:
```python
import functools
import itertools
import math

import jax
import jax.numpy as jnp
import numpy as np
from jax import lax
from jax.experimental import pallas as pl
from jax.experimental.pallas import tpu as pltpu
from jax.sharding import PartitionSpec as P

BAND = 50
LAGS = 16
CAP = 3
REACH = 4
COPIES = 2
EPSILON = 1e-05
LANES = 128
F32 = jnp.float32
BF16 = jnp.bfloat16
PICK_VMEM_LIMIT = 59 * 1024 * 1024
LAG_VMEM_LIMIT = 32 * 1024 * 1024

NT = (((1,), (1,)), ((), ()))


def dot_nt(left, right):
    return lax.dot_general(left, right, NT, preferred_element_type=F32)


def iota(shape, dim):
    return lax.broadcasted_iota(jnp.int32, shape, dim)


def send_keys(first, second, needs, sta_count, where):
    keys = []
    for reach in range(1, REACH):
        distance = abs((first + reach) % sta_count - first)
        shared = (needs >> reach) % 2 == 1
        first_sends = (first - second - reach) % sta_count == 0
        late = where(shared, where(first_sends, 2, 1), 0)
        keys.append((late * sta_count + distance) * REACH + reach)
    return keys


def read_pairs(pair_ref, owner_ref, block_count):
    pairs = []
    for pair in range(owner_ref.shape[0]):
        blocks = [pair_ref[side, pair] for side in range(2)]
        pairs.append((owner_ref[pair], blocks, [lax.div(block, block_count) for block in blocks]))
    return pairs


def case_of(pairs, case_ref, sta_count):
    first = second = needs = jnp.int32(0)
    for owner, _, homes in pairs:
        count = jnp.int32(0)
        for other, _, _ in pairs:
            count = count + (other == owner).astype(jnp.int32)
        ends = [lax.rem(home - owner + sta_count, sta_count) for home in homes]
        first = jnp.where(count == CAP, owner, first)
        second = jnp.where(count < CAP, owner, second)
        needs = jnp.where(count < CAP, (1 << ends[0]) | (1 << ends[1]), needs)
    return first, second, case_ref[case_number(first, second, needs, sta_count)]


def pick_kernel(kept, branched, sta_axis, pair_hbm, owner_hbm, member_hbm, case_hbm, x_ref, *rest):
    outs = rest[:REACH]
    branch_ref = rest[REACH] if branched else None
    pair_ref, owner_ref, member_ref, case_ref, x_buf, hot_buf, band_buf, y_buf, sems = rest[
        REACH + branched :
    ]
    freqs, tiles = x_buf.shape[0], x_buf.shape[2] // LANES
    step = freqs // COPIES
    block_count, width = member_ref.shape
    columns = y_buf.shape[1]
    chunks = columns // (2 * LANES)

    def fetch(part):
        rows = pl.ds(part * step, step)
        return pltpu.make_async_copy(x_ref.at[0, rows], x_buf.at[rows], sems.at[part])

    small = [
        pltpu.make_async_copy(source, target, sems.at[COPIES + index])
        for index, (source, target) in enumerate(
            (
                (pair_hbm, pair_ref),
                (owner_hbm, owner_ref),
                (member_hbm, member_ref),
                (case_hbm, case_ref),
            )
        )
    ]
    for copy in small:
        copy.start()
    for part in range(COPIES):
        fetch(part).start()

    row, col = iota((columns, LANES), 0), iota((columns, LANES), 1)
    low = (col % 16) * (2 * BAND)
    hit = (row >= low) & (row < low + 2 * BAND) & (row < 2 * freqs) & (col < 48)
    band_buf[...] = jnp.where(hit, 1.0, 0.0).astype(BF16)
    row, col = iota((2 * LANES, 2 * LANES), 0), iota((2 * LANES, 2 * LANES), 1)
    split = jnp.where(row == 2 * (col % LANES) + col // LANES, 1.0, 0.0).astype(BF16)
    y_buf[:, 2 * freqs :] = jnp.zeros((kept * width, columns - 2 * freqs), F32)
    for copy in small:
        copy.wait()

    my_sta = lax.axis_index(sta_axis)
    sta_count = lax.axis_size(sta_axis)
    members = jnp.transpose(member_ref[...].astype(F32))
    block_col = iota(members.shape, 1)
    pairs = read_pairs(pair_ref, owner_ref, block_count)
    found, wanted = jnp.int32(0), []
    for reach in range(REACH):
        owner = lax.rem(my_sta - reach + REACH * sta_count, sta_count)
        chosen = jnp.int32(-1)
        for pair_owner, blocks, homes in pairs:
            for block, home in zip(blocks, homes):
                hit = (pair_owner == owner) & (home == my_sta)
                chosen = jnp.where(hit, lax.rem(block, block_count), chosen)
        wanted.append((found, chosen))
        found = found + (chosen >= 0).astype(jnp.int32)
    places, station = [], []
    for place in range(kept):
        reach_here, block_here = jnp.int32(-1), jnp.int32(0)
        for reach, (rank, chosen) in enumerate(wanted):
            hit = (rank == place) & (chosen >= 0)
            reach_here = jnp.where(hit, reach, reach_here)
            block_here = jnp.where(hit, chosen, block_here)
        places.append(reach_here)
        column = jnp.where(block_col == block_here, members, 0.0)
        station.append(jnp.sum(column, axis=1, keepdims=True).astype(jnp.int32))
    station = jnp.concatenate(station, axis=0)
    lane = iota((kept * width, LANES), 1)
    for tile in range(tiles):
        hot = jnp.where(station == lane + tile * LANES, 1.0, 0.0).astype(BF16)
        hot_buf[:, tile * LANES : (tile + 1) * LANES] = hot

    if branched:
        branch_ref[0] = case_of(pairs, case_ref, sta_count)[2] >> REACH

    for part in range(COPIES):
        fetch(part).wait()
    x = jnp.concatenate(
        [
            x_buf[:, :, tile * LANES : (tile + 1) * LANES].reshape(2 * freqs, LANES)
            for tile in range(tiles)
        ],
        axis=1,
    )
    y_buf[:, : 2 * freqs] = dot_nt(hot_buf[:, : tiles * LANES], x)

    values = y_buf[...]
    square = values * values
    high = square.astype(BF16)
    low = (square - high.astype(F32)).astype(BF16)
    power = jnp.dot(high, band_buf[...], preferred_element_type=F32)
    power += jnp.dot(low, band_buf[...], preferred_element_type=F32)
    scale = lax.rsqrt(power * (1.0 / (2 * BAND)) + EPSILON)
    high = scale.astype(BF16)
    rest1 = scale - high.astype(F32)
    mid = rest1.astype(BF16)
    low = rest1 - mid.astype(F32)
    third = iota(scale.shape, 1) // 16
    pieces = jnp.where(
        third == 0, high.astype(F32), jnp.where(third == 1, mid.astype(F32), low)
    ).astype(BF16)
    white = (y_buf[...] * dot_nt(pieces, band_buf[...])).astype(BF16)
    parted = []
    for chunk in range(chunks):
        mixed = white[:, chunk * 2 * LANES : (chunk + 1) * 2 * LANES]
        parted.append(jnp.dot(mixed, split, preferred_element_type=F32).astype(BF16))
    white = jnp.concatenate(
        [part[:, :LANES] for part in parted] + [part[:, LANES:] for part in parted], axis=1
    )
    hot_buf[:, :columns] = white
    for place, reach_here in enumerate(places):
        for reach in range(REACH):

            @pl.when(reach_here == reach)
            def _():
                outs[reach][...] = hot_buf[place * width : (place + 1) * width, :columns]


def pick_blocks(kept, branched, spectra, pair_sides, pair_owner, block_members, case_table):
    _, freqs, parts, stations = spectra.shape
    block_count, width = block_members.shape
    columns = -(-freqs // LANES) * 2 * LANES
    rows = kept * width
    vmem = pl.BlockSpec(memory_space=pltpu.VMEM)
    smem = pl.BlockSpec(memory_space=pltpu.SMEM)
    out_shape = [jax.ShapeDtypeStruct((width, columns), BF16)] * REACH
    out_shape += [jax.ShapeDtypeStruct((1,), jnp.int32)] * branched
    return pl.pallas_call(
        functools.partial(pick_kernel, kept, branched, "sta"),
        out_shape=out_shape,
        in_specs=[pl.BlockSpec(memory_space=pltpu.HBM)] * 5,
        out_specs=[vmem] * REACH + [smem] * branched,
        scratch_shapes=[
            pltpu.SMEM(pair_sides.shape, jnp.int32),
            pltpu.SMEM(pair_owner.shape, jnp.int32),
            pltpu.VMEM(block_members.shape, jnp.int32),
            pltpu.SMEM(case_table.shape, jnp.int32),
            pltpu.VMEM((freqs, parts, stations), BF16),
            pltpu.VMEM((rows, max(columns, stations)), BF16),
            pltpu.VMEM((columns, LANES), BF16),
            pltpu.VMEM((rows, columns), F32),
            pltpu.SemaphoreType.DMA((COPIES + 4,)),
        ],
        compiler_params=pltpu.CompilerParams(vmem_limit_bytes=PICK_VMEM_LIMIT),
        cost_estimate=pl.CostEstimate(
            flops=2 * rows * stations * freqs * parts,
            bytes_accessed=2 * spectra.size + 4 * rows * columns,
            transcendentals=0,
        ),
        name="pick_and_whiten",
    )(pair_sides, pair_owner, block_members, case_table, spectra)


def case_number(first, second, needs, sta_count):
    return (first * sta_count + second) * (1 << (REACH - 1)) + needs // 2


def routes(sta_count):
    def load(first, second, sent):
        links = {}
        flows = [(first, reach) for reach in range(1, REACH)]
        flows += [(second, reach) for reach in range(1, REACH) if sent >> reach & 1]
        for owner, reach in flows:
            source = (owner + reach) % sta_count
            step = 1 if owner > source else -1
            for place in range(source, owner, step):
                links[place, step] = links.get((place, step), 0) + 1
        return max(links.values())

    every = (1 << REACH) - 2
    sets = [every] + [every - (1 << reach) for reach in range(REACH - 1, 0, -1)]
    branches = []
    cases = [0] * case_number(sta_count, 0, 0, sta_count)
    for first, second in itertools.permutations(range(sta_count), 2):
        for named in itertools.combinations(range(REACH), 2):
            needs = sum(1 << reach for reach in named) & every
            fits = [sent for sent in sets if needs & ~sent == 0]
            sent = min(fits, key=lambda sent: load(first, second, sent))
            branch = (first, second, sent)
            if branch not in branches:
                branches.append(branch)
            number = branches.index(branch)
            cases[case_number(first, second, needs, sta_count)] = (number << REACH) + sent
    return branches, cases


def phase_tables(sub_count, sub_freqs, groups, lag_rows):
    chunks = -(-sub_freqs // LANES)
    total = sub_count * sub_freqs
    freq = np.arange(total, dtype=np.int64).reshape(sub_count, 1, sub_freqs)
    middle = [2 * (group * lag_rows - LAGS // 2) + lag_rows - 1 for group in range(groups)]
    away = [step for step in range(1, lag_rows) if step % 2 != lag_rows % 2]

    def table(twice, forms, tile, dtype):
        twice = np.array(twice or [0], dtype=np.int64).reshape(1, -1, 1)
        angle = np.mod(freq * twice, 2 * total) * (math.pi / total)
        rows = np.stack([form(angle) for form in forms], axis=2)
        rows = rows.reshape(sub_count, -1, sub_freqs)
        pad = ((0, 0), (0, -rows.shape[1] % tile), (0, chunks * LANES - sub_freqs))
        return np.pad(rows, pad).astype(np.float32).astype(dtype)

    turns = table(middle, (np.cos, np.sin), 8, np.float32)
    offsets = table(away, (np.cos, np.sin, lambda angle: -np.sin(angle)), 16, BF16)
    return turns, offsets, len(away)


def lag_kernel(hops, slots, lag_rows, away, block_count, branched, pair_ref, owner_ref, case_ref, turn_ref, offset_ref, *refs):
    sub_count = lax.axis_size("sub")
    hr_count = lax.axis_size("hr")
    blocks = refs[: REACH * sub_count]
    outs = refs[REACH * sub_count : REACH * sub_count + len(hops)]
    buf, sems = refs[REACH * sub_count + len(hops) :]
    width = buf.shape[1]
    span = buf.shape[2] // 2
    middle_lag = lag_rows % 2
    my_sub = lax.axis_index("sub")
    my_hr = lax.axis_index("hr")
    my_sta = lax.axis_index("sta")
    sta_count = lax.axis_size("sta")

    pairs = read_pairs(pair_ref, owner_ref, block_count)
    order = [jnp.int32(reach) for reach in range(REACH)]
    if branched:
        first, second, case = case_of(pairs, case_ref, sta_count)
        keys = send_keys(first, second, case, sta_count, jnp.where)
        for reach, key in enumerate(keys):
            order[1 + reach] = 1 + sum((other < key).astype(jnp.int32) for other in keys)
    owned = []
    for owner, _, homes in pairs:
        places = []
        for home in homes:
            reach_here = lax.rem(home - my_sta + sta_count, sta_count)
            place_here = order[0]
            for reach in range(1, REACH):
                place_here = jnp.where(reach_here == reach, order[reach], place_here)
            places.append(place_here)
        owned.append((owner == my_sta, places))
    ends = []
    for slot in slots:
        count = jnp.int32(0)
        slot_ends = [jnp.int32(-1)] * 2
        for mine, places in owned:
            hit = mine & (count == slot)
            count = count + mine.astype(jnp.int32)
            slot_ends = [jnp.where(hit, new, old) for new, old in zip(places, slot_ends)]
        ends.append(slot_ends)

    def fetch(place, step):
        piece = place * sub_count + step
        return pltpu.make_async_copy(blocks[piece], buf.at[piece], sems.at[piece])

    pieces = [(place, step) for step in range(sub_count) for place in range(REACH)]

    @pl.when(ends[0][0] >= 0)
    def _():
        for place, step in pieces:
            fetch(place, step).start()

    for index, (left, right) in enumerate(ends):

        @pl.when(left < 0)
        def _():
            for out in outs:
                out[:, index] = jnp.zeros((lag_rows, width, width), out.dtype)

        @pl.when(left >= 0)
        def _():
            total = None
            for step in range(sub_count):
                if index == 0:
                    for place in range(REACH):
                        fetch(place, step).wait()
                sub = lax.rem(my_sub + step, sub_count)
                real = buf[left * sub_count + step, :, :span]
                imag = buf[left * sub_count + step, :, span:]
                scaled_real, scaled_imag = [real] * middle_lag, [imag] * middle_lag
                for near in range(away):
                    cosine, sine, minus = (
                        offset_ref[sub, 3 * near + form : 3 * near + form + 1, :]
                        for form in range(3)
                    )
                    scaled_real += [real * cosine, imag * minus]
                    scaled_imag += [imag * cosine, real * sine]
                real = buf[right * sub_count + step, :, :span].astype(F32)
                imag = buf[right * sub_count + step, :, span:].astype(F32)
                turned_real, turned_imag = [], []
                for hop in hops:
                    group = lax.rem(my_hr + hop, hr_count) * sub_count + my_sub
                    cosine = turn_ref[sub, pl.ds(2 * group, 1), :]
                    sine = turn_ref[sub, pl.ds(2 * group + 1, 1), :]
                    turned_real.append((real * cosine + imag * sine).astype(BF16))
                    turned_imag.append((imag * cosine - real * sine).astype(BF16))
                for scaled, turned in ((scaled_real, turned_real), (scaled_imag, turned_imag)):
                    part = dot_nt(jnp.concatenate(scaled, axis=0), jnp.concatenate(turned, axis=0))
                    total = part if total is None else total + part
            for place, out in enumerate(outs):
                columns = slice(place * width, (place + 1) * width)
                if middle_lag:
                    out[lag_rows // 2, index] = total[:width, columns].astype(out.dtype)
                for near in range(away):
                    start = (middle_lag + 2 * near) * width
                    even = total[start : start + width, columns]
                    odd = total[start + width : start + 2 * width, columns]
                    below = (lag_rows - 1) // 2 - near - middle_lag
                    above = lag_rows - 1 - below
                    out[above, index] = (even + odd).astype(out.dtype)
                    out[below, index] = (even - odd).astype(out.dtype)


def on_device(spectra, pair_blocks, pair_owner, block_members):
    hour_count, sub_freqs, _, _ = spectra.shape
    block_count, width = block_members.shape
    sta_count, hr_count, sub_count = (lax.axis_size(axis) for axis in ("sta", "hr", "sub"))
    groups = hr_count * sub_count
    lag_rows = LAGS // groups
    norming = 1.0 / math.sqrt(hour_count * hr_count * sub_count * sub_freqs)
    pair_sides = pair_blocks.T
    turns, offsets, away = phase_tables(sub_count, sub_freqs, groups, lag_rows)

    owners_at_most = pair_owner.shape[0] - CAP + 1
    branched = owners_at_most == 2 and sta_count == REACH
    kept = min(REACH, owners_at_most)
    branches, cases = routes(sta_count) if branched else ([], [])
    case_table = jnp.asarray(np.array(cases or [0], dtype=np.int32))
    picked = pick_blocks(
        kept, branched, spectra, pair_sides, pair_owner, block_members, case_table
    )

    def exchange(owners_of, order, *picked):
        arrived = [picked[0]]
        for reach in order:
            to_owner = [((owner + reach) % sta_count, owner) for owner in owners_of[reach - 1]]
            arrived.append(lax.ppermute(picked[reach], "sta", to_owner))
        blocks = []
        for block in arrived:
            blocks.append(block)
            for step in range(1, sub_count):
                swap = [((sub + step) % sub_count, sub) for sub in range(sub_count)]
                blocks.append(lax.ppermute(block, "sub", swap))
        return blocks

    if branched:
        steps = []
        for first, second, sent in branches:
            owners_of = [
                (first, second) if sent >> reach & 1 else (first,) for reach in range(1, REACH)
            ]
            keys = send_keys(first, second, sent, sta_count, lambda hit, yes, no: yes if hit else no)
            order = sorted(range(1, REACH), key=lambda reach: keys[reach - 1])
            steps.append(functools.partial(exchange, owners_of, order))
        blocks = lax.switch(picked[REACH][0], steps, *picked[:REACH])
    else:
        blocks = exchange([range(sta_count)] * (REACH - 1), range(1, REACH), *picked[:REACH])

    smem = pl.BlockSpec(memory_space=pltpu.SMEM)
    vmem = pl.BlockSpec(memory_space=pltpu.VMEM)
    hbm = pl.BlockSpec(memory_space=pltpu.HBM)
    row = picked[0].shape[1]
    versions = (lag_rows % 2 + 2 * away) * width

    def products(hops, slots, dtype, name):
        return pl.pallas_call(
            functools.partial(
                lag_kernel, hops, slots, lag_rows, away, block_count, branched
            ),
            out_shape=[jax.ShapeDtypeStruct((lag_rows, len(slots), width, width), dtype)]
            * len(hops),
            in_specs=[smem, smem, smem, vmem, vmem] + [hbm] * len(blocks),
            out_specs=[vmem] * len(hops),
            scratch_shapes=[
                pltpu.VMEM((len(blocks), width, row), BF16),
                pltpu.SemaphoreType.DMA((len(blocks),)),
            ],
            compiler_params=pltpu.CompilerParams(vmem_limit_bytes=LAG_VMEM_LIMIT),
            cost_estimate=pl.CostEstimate(
                flops=2 * len(slots) * len(hops) * versions * width * sub_count * row,
                bytes_accessed=2 * len(blocks) * width * row,
                transcendentals=0,
            ),
            name=name,
        )(pair_sides, pair_owner, case_table, turns, offsets, *blocks)

    hops, slots = tuple(range(1, hr_count)), tuple(range(CAP))
    sent = products(hops, slots, BF16, "lags_to_send")
    received = []
    for hop, part in zip(hops, sent):
        to_device = [(hr, (hr + hop) % hr_count) for hr in range(hr_count)]
        received.append(lax.ppermute(part, "hr", to_device))
    (summed,) = products((0,), slots, F32, "lags_to_keep")
    for part in received:
        summed = summed + part.astype(F32)
    return (summed * norming).astype(BF16)


def solution(mesh):
    placed = (P(("grp", "hr"), "sub", None, "sta"), P(), P(), P("sta", None))
    return jax.shard_map(
        on_device,
        mesh=mesh,
        in_specs=placed,
        out_specs=P(("grp", "hr", "sub"), "sta", None, None),
        check_vma=False,
    )
```

profile of v0, /device:TPU:18, one launch (start us, length us, event | category | flops | bytes accessed | tf_op | source)
XLA Modules:
  0.0 45.9 jit_solution(13324451762831000103)
XLA Ops:
  0.0 0.0 copy-start.1
  0.0 0.0 copy-start
  0.0 4.1 %pick_and_whiten.1 = (bf16[128,1024]{1,0:T(8,128)(2,1)S(1)}, bf16[128,1024]{1,0:T(8,128)(2,1)S(1)}, bf16[128,1024]{1,0:T(8,128)(2,1)S(1)}, bf16[128,1024]{1,0:T(8,128)(2,1)S(1)}, s32[1]{0:T(128)}) custom-call(s32[2,4]{1,0:T(2,128)} %bitcast.2, s32[4]{0:T(128)} %owner_ref.3, s32[8,128]{1,0:T(8,128)} %member_hbm.1, s32[128]{0:T(128)} %constant.14.clone.case_hbm.case_ref, ...), custom_call_target="tpu_custom_call" | custom-call | flops 524288000 | bytes 3096576 | tf_op jit(solution)/shard_map/pick_and_whiten/pallas_call | solution.py:196
  4.8 24.1 %conditional.1 = (bf16[128,1024]{1,0:T(8,128)(2,1)}, bf16[128,1024]{1,0:T(8,128)(2,1)}, bf16[128,1024]{1,0:T(8,128)(2,1)}, bf16[128,1024]{1,0:T(8,128)(2,1)}, bf...) conditional(s32[]{:T(128)} %bitcast.1, ...), branch_computations={%region_0.0_spmd, %region_1.0_spmd, %region_2.0_spmd, %region_3.0_... | conditional | bytes 7340368 | solution.py:419
  4.8 1.3 %collective-permute-start.113 = (bf16[128,1024]{1,0:T(8,128)(2,1)S(1)}, bf16[128,1024]{1,0:T(8,128)(2,1)}, u32[]{:S(2)}, u32[]{:S(2)}) collective-permute-start(bf16[128,1024]{1,0:T(8,128)(2,1)S(1)} %get-tuple-element.262), channel_id=1, source_target_pairs={{0,8},{1,9},{2,10},{3,11},{16,24},{17,25},{18,26},{19,27}} | collective-permute-start | bytes 786440 | tf_op jit(solution)/shard_map/cond/branch_16_fun/ppermute | solution.py:401
  6.1 1.3 %collective-permute-start.115 = (bf16[128,1024]{1,0:T(8,128)(2,1)S(1)}, bf16[128,1024]{1,0:T(8,128)(2,1)}, u32[]{:S(2)}, u32[]{:S(2)}) collective-permute-start(bf16[128,1024]{1,0:T(8,128)(2,1)S(1)} %get-tuple-element.263), channel_id=1, source_target_pairs={{12,8},{0,12},{13,9},{1,13},{14,10},{2,14},{15,11},{3,15},{28,24},... | collective-permute-start | bytes 786440 | tf_op jit(solution)/shard_map/cond/branch_16_fun/ppermute | solution.py:401
  7.4 4.6 %collective-permute-start.117 = (bf16[128,1024]{1,0:T(8,128)(2,1)S(1)}, bf16[128,1024]{1,0:T(8,128)(2,1)}, u32[]{:S(2)}, u32[]{:S(2)}) collective-permute-start(bf16[128,1024]{1,0:T(8,128)(2,1)S(1)} %get-tuple-element.264), channel_id=1, source_target_pairs={{4,8},{8,12},{5,9},{9,13},{6,10},{10,14},{7,11},{11,15},{20,24},{2... | collective-permute-start | bytes 786440 | tf_op jit(solution)/shard_map/cond/branch_16_fun/ppermute | solution.py:401
  12.0 0.1 collective-permute-start.112
  12.1 5.0 %collective-permute-done.113 = bf16[128,1024]{1,0:T(8,128)(2,1)} collective-permute-done((bf16[128,1024]{1,0:T(8,128)(2,1)S(1)}, bf16[128,1024]{1,0:T(8,128)(2,1)}, u32[]{:S(2)}, u32[]{:S(2)}) %collective-permute-start.113) | collective-permute-done | bytes 262176 | tf_op jit(solution)/shard_map/cond/branch_16_fun/ppermute | solution.py:401
  17.0 0.0 collective-permute-start.114
  17.0 0.0 collective-permute-done.115
  17.0 0.5 %collective-permute-start.116 = (bf16[128,1024]{1,0:T(8,128)(2,1)}, bf16[128,1024]{1,0:T(8,128)(2,1)}, u32[]{:S(2)}, u32[]{:S(2)}) collective-permute-start(bf16[128,1024]{1,0:T(8,128)(2,1)} %collective-permute-done.115), channel_id=1, source_target_pairs={{1,0},{0,1},{3,2},{2,3},{5,4},{4,5},{7,6},{6,7},{9,8},{8,9},{11,10... | collective-permute-start | bytes 786440 | tf_op jit(solution)/shard_map/cond/branch_16_fun/ppermute | solution.py:407
  17.5 9.5 %collective-permute-done.117 = bf16[128,1024]{1,0:T(8,128)(2,1)} collective-permute-done((bf16[128,1024]{1,0:T(8,128)(2,1)S(1)}, bf16[128,1024]{1,0:T(8,128)(2,1)}, u32[]{:S(2)}, u32[]{:S(2)}) %collective-permute-start.117) | collective-permute-done | bytes 262176 | tf_op jit(solution)/shard_map/cond/branch_16_fun/ppermute | solution.py:401
  27.0 0.0 collective-permute-start.118
  27.0 0.0 collective-permute-done.112
  27.0 0.0 collective-permute-done.114
  27.0 0.0 collective-permute-done.116
  27.1 1.8 %collective-permute-done.118 = bf16[128,1024]{1,0:T(8,128)(2,1)} collective-permute-done((bf16[128,1024]{1,0:T(8,128)(2,1)}, bf16[128,1024]{1,0:T(8,128)(2,1)}, u32[]{:S(2)}, u32[]{:S(2)}) %collective-permute-start.118) | collective-permute-done | bytes 262176 | tf_op jit(solution)/shard_map/cond/branch_16_fun/ppermute | solution.py:407
  28.9 0.0 copy-done.2
  28.9 4.8 %lags_to_send.1 = bf16[4,3,128,128]{3,2,1,0:T(8,128)(2,1)S(1)} custom-call(s32[2,4]{1,0:T(2,128)S(1)} %bitcast.3, s32[4]{0:T(128)S(1)} %copy-done.1, s32[128]{0:T(128)S(1)} %copy-done.2, f32[2,8,512]{2,1,0:T(8,128)S(1)} %copy-done.4, bf16[2,16,512]{2,1,0:T(8,128)(2,1)S(1)} %copy-done.3, bf16[128,1024]{1,0:T(8,128)(2,1)S(1)} %get-tuple-element.305.refs_0_, ...), custom_call_target="tpu_custom_call" | custom-call | flops 805306368 | bytes 2097152 | tf_op jit(solution)/shard_map/lags_to_send/pallas_call | solution.py:430
  33.8 0.6 %collective-permute-start.168 = (bf16[4,3,128,128]{3,2,1,0:T(8,128)(2,1)S(1)}, bf16[4,3,128,128]{3,2,1,0:T(8,128)(2,1)S(1)}, u32[]{:S(2)}, u32[]{:S(2)}) collective-permute-start(bf16[4,3,128,128]{3,2,1,0:T(8,128)(2,1)S(1)} %lags_to_send.1), channel_id=1, source_target_pairs={{0,2},{2,0},{1,3},{3,1},{4,6},{6,4},{5,7},{7,5},{8,10},{10,8},{9,1... | collective-permute-start | bytes 1179656 | tf_op jit(solution)/shard_map/ppermute | solution.py:456
  34.4 4.8 %lags_to_keep.1 = f32[4,3,128,128]{3,2,1,0:T(8,128)S(1)} custom-call(s32[2,4]{1,0:T(2,128)S(1)} %bitcast.4, s32[4]{0:T(128)S(1)} %copy-done.1, s32[128]{0:T(128)S(1)} %copy-done.2, f32[2,8,512]{2,1,0:T(8,128)S(1)} %copy-done.4, bf16[2,16,512]{2,1,0:T(8,128)(2,1)S(1)} %copy-done.3, bf16[128,1024]{1,0:T(8,128)(2,1)S(1)} %get-tuple-element.305.refs_0_, ...), custom_call_target="tpu_custom_call" | custom-call | flops 805306368 | bytes 2097152 | tf_op jit(solution)/shard_map/lags_to_keep/pallas_call | solution.py:430
  39.2 5.8 %collective-permute-done.168 = bf16[4,3,128,128]{3,2,1,0:T(8,128)(2,1)S(1)} collective-permute-done((bf16[4,3,128,128]{3,2,1,0:T(8,128)(2,1)S(1)}, bf16[4,3,128,128]{3,2,1,0:T(8,128)(2,1)S(1)}, u32[]{:S(2)}, u32[]{:S(2)}) %collective-permute-start.168) | collective-permute-done | bytes 393248 | tf_op jit(solution)/shard_map/ppermute | solution.py:456
  45.0 0.9 %multiply_convert_fusion = bf16[4,3,128,128]{3,2,1,0:T(8,128)(2,1)} fusion(f32[4,3,128,128]{3,2,1,0:T(8,128)S(1)} %lags_to_keep.1, bf16[4,3,128,128]{3,2,1,0:T(8,128)(2,1)S(1)} %collective-permute-done.168), kind=kLoop, calls=%fused_computation | loop fusion | flops 786432 | bytes 1572864 | tf_op jit(solution)/shard_map/convert_element_type | solution.py:460
  (7 shorter events, 0.0 us)
Async XLA Ops:
  0.0 28.9 %copy-start.2 = (s32[128]{0:T(128)S(1)}, s32[128]{0:T(128)}, u32[]{:S(2)}) copy-start(s32[128]{0:T(128)} %constant.14.clone.case_hbm.case_ref) | copy-start | bytes 1540
  0.0 28.9 %copy-start.3 = (bf16[2,16,512]{2,1,0:T(8,128)(2,1)S(1)}, bf16[2,16,512]{2,1,0:T(8,128)(2,1)}, u32[]{:S(2)}) copy-start(bf16[2,16,512]{2,1,0:T(8,128)(2,1)} %constant.16.clone.offset_ref) | copy-start | bytes 98308
  0.0 28.9 %copy-start.4 = (f32[2,8,512]{2,1,0:T(8,128)S(1)}, f32[2,8,512]{2,1,0:T(8,128)}, u32[]{:S(2)}) copy-start(f32[2,8,512]{2,1,0:T(8,128)} %constant.15.clone.turn_ref) | copy-start | bytes 98308
  0.0 28.9 %copy-start.1 = (s32[4]{0:T(128)S(1)}, s32[4]{0:T(128)}, u32[]{:S(2)}) copy-start(s32[4]{0:T(128)} %owner_ref.3) | copy-start | bytes 52
  0.0 28.9 %copy-start = (s32[4,2]{0,1:T(2,128)S(1)}, s32[4,2]{0,1:T(2,128)}, u32[]{:S(2)}) copy-start(s32[4,2]{0,1:T(2,128)} %param.32) | copy-start | bytes 100
  4.8 12.2 %collective-permute-start.113 = (bf16[128,1024]{1,0:T(8,128)(2,1)S(1)}, bf16[128,1024]{1,0:T(8,128)(2,1)}, u32[]{:S(2)}, u32[]{:S(2)}) collective-permute-start(bf16[128,1024]{1,0:T(8,128)(2,1)S(1)} %get-tuple-element.262), channel_id=1, source_target_pairs={{0,8},{1,9},{2,10},{3,11},{16,24},{17,25},{18,26},{19,27}} | collective-permute-start | bytes 786440 | tf_op jit(solution)/shard_map/cond/branch_16_fun/ppermute | solution.py:401
  6.1 10.9 %collective-permute-start.115 = (bf16[128,1024]{1,0:T(8,128)(2,1)S(1)}, bf16[128,1024]{1,0:T(8,128)(2,1)}, u32[]{:S(2)}, u32[]{:S(2)}) collective-permute-start(bf16[128,1024]{1,0:T(8,128)(2,1)S(1)} %get-tuple-element.263), channel_id=1, source_target_pairs={{12,8},{0,12},{13,9},{1,13},{14,10},{2,14},{15,11},{3,15},{28,24},... | collective-permute-start | bytes 786440 | tf_op jit(solution)/shard_map/cond/branch_16_fun/ppermute | solution.py:401
  7.4 19.6 %collective-permute-start.117 = (bf16[128,1024]{1,0:T(8,128)(2,1)S(1)}, bf16[128,1024]{1,0:T(8,128)(2,1)}, u32[]{:S(2)}, u32[]{:S(2)}) collective-permute-start(bf16[128,1024]{1,0:T(8,128)(2,1)S(1)} %get-tuple-element.264), channel_id=1, source_target_pairs={{4,8},{8,12},{5,9},{9,13},{6,10},{10,14},{7,11},{11,15},{20,24},{2... | collective-permute-start | bytes 786440 | tf_op jit(solution)/shard_map/cond/branch_16_fun/ppermute | solution.py:401
  12.0 15.0 %collective-permute-start.112 = (bf16[128,1024]{1,0:T(8,128)(2,1)S(1)}, bf16[128,1024]{1,0:T(8,128)(2,1)}, u32[]{:S(2)}, u32[]{:S(2)}) collective-permute-start(bf16[128,1024]{1,0:T(8,128)(2,1)S(1)} %get-tuple-element.261), channel_id=1, source_target_pairs={{1,0},{0,1},{3,2},{2,3},{5,4},{4,5},{7,6},{6,7},{9,8},{8,9},{11,10... | collective-permute-start | bytes 786440 | tf_op jit(solution)/shard_map/cond/branch_16_fun/ppermute | solution.py:407
  17.0 10.0 %collective-permute-start.114 = (bf16[128,1024]{1,0:T(8,128)(2,1)}, bf16[128,1024]{1,0:T(8,128)(2,1)}, u32[]{:S(2)}, u32[]{:S(2)}) collective-permute-start(bf16[128,1024]{1,0:T(8,128)(2,1)} %collective-permute-done.113), channel_id=1, source_target_pairs={{1,0},{0,1},{3,2},{2,3},{5,4},{4,5},{7,6},{6,7},{9,8},{8,9},{11,10... | collective-permute-start | bytes 786440 | tf_op jit(solution)/shard_map/cond/branch_16_fun/ppermute | solution.py:407
  17.0 10.0 %collective-permute-start.116 = (bf16[128,1024]{1,0:T(8,128)(2,1)}, bf16[128,1024]{1,0:T(8,128)(2,1)}, u32[]{:S(2)}, u32[]{:S(2)}) collective-permute-start(bf16[128,1024]{1,0:T(8,128)(2,1)} %collective-permute-done.115), channel_id=1, source_target_pairs={{1,0},{0,1},{3,2},{2,3},{5,4},{4,5},{7,6},{6,7},{9,8},{8,9},{11,10... | collective-permute-start | bytes 786440 | tf_op jit(solution)/shard_map/cond/branch_16_fun/ppermute | solution.py:407
  27.0 1.9 %collective-permute-start.118 = (bf16[128,1024]{1,0:T(8,128)(2,1)}, bf16[128,1024]{1,0:T(8,128)(2,1)}, u32[]{:S(2)}, u32[]{:S(2)}) collective-permute-start(bf16[128,1024]{1,0:T(8,128)(2,1)} %collective-permute-done.117), channel_id=1, source_target_pairs={{1,0},{0,1},{3,2},{2,3},{5,4},{4,5},{7,6},{6,7},{9,8},{8,9},{11,10... | collective-permute-start | bytes 786440 | tf_op jit(solution)/shard_map/cond/branch_16_fun/ppermute | solution.py:407
  33.8 11.2 %collective-permute-start.168 = (bf16[4,3,128,128]{3,2,1,0:T(8,128)(2,1)S(1)}, bf16[4,3,128,128]{3,2,1,0:T(8,128)(2,1)S(1)}, u32[]{:S(2)}, u32[]{:S(2)}) collective-permute-start(bf16[4,3,128,128]{3,2,1,0:T(8,128)(2,1)S(1)} %lags_to_send.1), channel_id=1, source_target_pairs={{0,2},{2,0},{1,3},{3,1},{4,6},{6,4},{5,7},{7,5},{8,10},{10,8},{9,1... | collective-permute-start | bytes 1179656 | tf_op jit(solution)/shard_map/ppermute | solution.py:456
where the time goes:
time: 46.7 us; the launch traced here: 45.9 us
  waiting for transfers between devices  22.1 us (47%)
  Pallas kernels  13.8 us (30%)
  starting transfers between devices  8.33 us (18%)
  other arithmetic  0.86 us (2%)
  between operations  0.72 us (2%)
    ppermute x3, waiting for transfers between devices, exchange(): arrived.append(lax.ppermute(picked[reach], 'sta', to_owner))  14.4 us
    pallas_call x2, Pallas kernels, products(): pl.pallas_call(functools.partial(lag_kernel, hops, slots, lag_rows, away,...  9.65 us
    ppermute x3, starting transfers between devices, exchange(): arrived.append(lax.ppermute(picked[reach], 'sta', to_owner))  7.14 us
    ppermute x1, waiting for transfers between devices, on_device(): received.append(lax.ppermute(part, 'hr', to_device))  5.8 us
    pallas_call x1, Pallas kernels, pick_blocks(): pl.pallas_call(functools.partial(pick_kernel, kept, branched, 'sta'), out...  4.12 us
    ppermute x4, waiting for transfers between devices, exchange(): blocks.append(lax.ppermute(block, 'sub', swap))  1.86 us
  transfers between devices with their start and end apart: 8, of which 4 were waited for; matrix products, arithmetic and copies ran while one was open for 0% of the time, Pallas kernels for 10%

commit v1 on v0

--- a/solution.py
+++ b/solution.py
@@ -14,7 +14,6 @@
 LAGS = 16
 CAP = 3
 REACH = 4
-COPIES = 2
 EPSILON = 1e-05
 LANES = 128
 F32 = jnp.float32
@@ -72,17 +71,18 @@
         REACH + branched :
     ]
     freqs, tiles = x_buf.shape[0], x_buf.shape[2] // LANES
-    step = freqs // COPIES
     block_count, width = member_ref.shape
     columns = y_buf.shape[1]
     chunks = columns // (2 * LANES)
 
+    runs = [(first, min(LANES, freqs - first)) for first in range(0, freqs, LANES)]
+
     def fetch(part):
-        rows = pl.ds(part * step, step)
+        rows = pl.ds(*runs[part])
         return pltpu.make_async_copy(x_ref.at[0, rows], x_buf.at[rows], sems.at[part])
 
     small = [
-        pltpu.make_async_copy(source, target, sems.at[COPIES + index])
+        pltpu.make_async_copy(source, target, sems.at[len(runs) + index])
         for index, (source, target) in enumerate(
             (
                 (pair_hbm, pair_ref),
@@ -94,7 +94,7 @@
     ]
     for copy in small:
         copy.start()
-    for part in range(COPIES):
+    for part in range(len(runs)):
         fetch(part).start()
 
     row, col = iota((columns, LANES), 0), iota((columns, LANES), 1)
@@ -141,16 +141,18 @@
     if branched:
         branch_ref[0] = case_of(pairs, case_ref, sta_count)[2] >> REACH
 
-    for part in range(COPIES):
+    for part, (first, count) in enumerate(runs):
         fetch(part).wait()
-    x = jnp.concatenate(
-        [
-            x_buf[:, :, tile * LANES : (tile + 1) * LANES].reshape(2 * freqs, LANES)
-            for tile in range(tiles)
-        ],
-        axis=1,
-    )
-    y_buf[:, : 2 * freqs] = dot_nt(hot_buf[:, : tiles * LANES], x)
+        x = jnp.concatenate(
+            [
+                x_buf[first : first + count, :, tile * LANES : (tile + 1) * LANES].reshape(
+                    2 * count, LANES
+                )
+                for tile in range(tiles)
+            ],
+            axis=1,
+        )
+        y_buf[:, 2 * first : 2 * (first + count)] = dot_nt(hot_buf[:, : tiles * LANES], x)
 
     values = y_buf[...]
     square = values * values
@@ -207,7 +209,7 @@
             pltpu.VMEM((rows, max(columns, stations)), BF16),
             pltpu.VMEM((columns, LANES), BF16),
             pltpu.VMEM((rows, columns), F32),
-            pltpu.SemaphoreType.DMA((COPIES + 4,)),
+            pltpu.SemaphoreType.DMA((-(-freqs // LANES) + 4,)),
         ],
         compiler_params=pltpu.CompilerParams(vmem_limit_bytes=PICK_VMEM_LIMIT),
         cost_estimate=pl.CostEstimate(
@@ -313,16 +315,30 @@
             slot_ends = [jnp.where(hit, new, old) for new, old in zip(places, slot_ends)]
         ends.append(slot_ends)
 
-    def fetch(place, step):
-        piece = place * sub_count + step
-        return pltpu.make_async_copy(blocks[piece], buf.at[piece], sems.at[piece])
-
-    pieces = [(place, step) for step in range(sub_count) for place in range(REACH)]
-
-    @pl.when(ends[0][0] >= 0)
-    def _():
-        for place, step in pieces:
-            fetch(place, step).start()
+    fresh, seen = [], []
+    for place in itertools.chain.from_iterable(ends):
+        known = place < 0
+        for other in seen:
+            known = known | (other == place)
+        seen.append(place)
+        fresh.append(jnp.logical_not(known))
+    for slot_pair in range(0, len(seen), 2):
+        for step in range(sub_count):
+            for entry in (slot_pair, slot_pair + 1):
+                for place in range(REACH):
+
+                    @pl.when(fresh[entry] & (seen[entry] == place))
+                    def _():
+                        piece = place * sub_count + step
+                        pltpu.make_async_copy(
+                            blocks[piece], buf.at[piece], sems.at[piece]
+                        ).start()
+
+    def arrive(entry, step):
+        @pl.when(fresh[entry])
+        def _():
+            piece = seen[entry] * sub_count + step
+            pltpu.make_async_copy(blocks[step], buf.at[piece], sems.at[piece]).wait()
 
     for index, (left, right) in enumerate(ends):
 
@@ -335,9 +351,8 @@
         def _():
             total = None
             for step in range(sub_count):
-                if index == 0:
-                    for place in range(REACH):
-                        fetch(place, step).wait()
+                arrive(2 * index, step)
+                arrive(2 * index + 1, step)
                 sub = lax.rem(my_sub + step, sub_count)
                 real = buf[left * sub_count + step, :, :span]
                 imag = buf[left * sub_count + step, :, span:]

time: 46.7 us -> 48.5 us (1.039)
  the two profiles are of different devices: /device:TPU:18 before, /device:TPU:30 now
where the time goes in v1:
time: 48.5 us; the launch traced here: 48 us
  waiting for transfers between devices  21.3 us (44%)
  Pallas kernels  16.6 us (34%)
  starting transfers between devices  8.31 us (17%)
  other arithmetic  0.86 us (2%)
  between operations  0.72 us (1%)
    ppermute x3, waiting for transfers between devices, exchange(): arrived.append(lax.ppermute(picked[reach], 'sta', to_owner))  14.9 us
    pallas_call x2, Pallas kernels, products(): pl.pallas_call(functools.partial(lag_kernel, hops, slots, lag_rows, away,...  12.1 us
    ppermute x3, starting transfers between devices, exchange(): arrived.append(lax.ppermute(picked[reach], 'sta', to_owner))  7.14 us
    ppermute x1, waiting for transfers between devices, on_device(): received.append(lax.ppermute(part, 'hr', to_device))  4.6 us
    pallas_call x1, Pallas kernels, pick_blocks(): pl.pallas_call(functools.partial(pick_kernel, kept, branched, 'sta'), out...  4.52 us
    ppermute x4, waiting for transfers between devices, exchange(): blocks.append(lax.ppermute(block, 'sub', swap))  1.74 us
  transfers between devices with their start and end apart: 8, of which 5 were waited for; matrix products, arithmetic and copies ran while one was open for 0% of the time, Pallas kernels for 13%

profile of v1, /device:TPU:30, one launch (start us, length us, event | category | flops | bytes accessed | tf_op | source)
XLA Modules:
  0.0 48.0 jit_solution(5404195064726619996)
XLA Ops:
  0.0 0.0 copy-start.1
  0.0 0.0 copy-start
  0.0 4.5 %pick_and_whiten.1 = (bf16[128,1024]{1,0:T(8,128)(2,1)S(1)}, bf16[128,1024]{1,0:T(8,128)(2,1)S(1)}, bf16[128,1024]{1,0:T(8,128)(2,1)S(1)}, bf16[128,1024]{1,0:T(8,128)(2,1)S(1)}, s32[1]{0:T(128)}) custom-call(s32[2,4]{1,0:T(2,128)} %bitcast.2, s32[4]{0:T(128)} %owner_ref.3, s32[8,128]{1,0:T(8,128)} %member_hbm.1, s32[128]{0:T(128)} %constant.14.clone.case_hbm.case_ref, ...), custom_call_target="tpu_custom_call" | custom-call | flops 524288000 | bytes 3096576 | tf_op jit(solution)/shard_map/pick_and_whiten/pallas_call | solution.py:198
  5.2 24.7 %conditional.1 = (bf16[128,1024]{1,0:T(8,128)(2,1)}, bf16[128,1024]{1,0:T(8,128)(2,1)}, bf16[128,1024]{1,0:T(8,128)(2,1)}, bf16[128,1024]{1,0:T(8,128)(2,1)}, bf...) conditional(s32[]{:T(128)} %bitcast.1, ...), branch_computations={%region_0.0_spmd, %region_1.0_spmd, %region_2.0_spmd, %region_3.0_... | conditional | bytes 7340368 | solution.py:434
  5.4 1.3 %collective-permute-start.155 = (bf16[128,1024]{1,0:T(8,128)(2,1)S(1)}, bf16[128,1024]{1,0:T(8,128)(2,1)}, u32[]{:S(2)}, u32[]{:S(2)}) collective-permute-start(bf16[128,1024]{1,0:T(8,128)(2,1)S(1)} %get-tuple-element.286), channel_id=1, source_target_pairs={{4,12},{5,13},{6,14},{7,15},{20,28},{21,29},{22,30},{23,31}} | collective-permute-start | bytes 786440 | tf_op jit(solution)/shard_map/cond/branch_22_fun/ppermute | solution.py:416
  6.7 1.3 %collective-permute-start.157 = (bf16[128,1024]{1,0:T(8,128)(2,1)S(1)}, bf16[128,1024]{1,0:T(8,128)(2,1)}, u32[]{:S(2)}, u32[]{:S(2)}) collective-permute-start(bf16[128,1024]{1,0:T(8,128)(2,1)S(1)} %get-tuple-element.287), channel_id=1, source_target_pairs={{8,12},{4,8},{9,13},{5,9},{10,14},{6,10},{11,15},{7,11},{24,28},{2... | collective-permute-start | bytes 786440 | tf_op jit(solution)/shard_map/cond/branch_22_fun/ppermute | solution.py:416
  8.0 4.6 %collective-permute-start.159 = (bf16[128,1024]{1,0:T(8,128)(2,1)S(1)}, bf16[128,1024]{1,0:T(8,128)(2,1)}, u32[]{:S(2)}, u32[]{:S(2)}) collective-permute-start(bf16[128,1024]{1,0:T(8,128)(2,1)S(1)} %get-tuple-element.288), channel_id=1, source_target_pairs={{0,12},{12,8},{1,13},{13,9},{2,14},{14,10},{3,15},{15,11},{16,28},... | collective-permute-start | bytes 786440 | tf_op jit(solution)/shard_map/cond/branch_22_fun/ppermute | solution.py:416
  12.6 0.1 collective-permute-start.154
  12.7 10.5 %collective-permute-done.155 = bf16[128,1024]{1,0:T(8,128)(2,1)} collective-permute-done((bf16[128,1024]{1,0:T(8,128)(2,1)S(1)}, bf16[128,1024]{1,0:T(8,128)(2,1)}, u32[]{:S(2)}, u32[]{:S(2)}) %collective-permute-start.155) | collective-permute-done | bytes 262176 | tf_op jit(solution)/shard_map/cond/branch_22_fun/ppermute | solution.py:416
  23.2 0.0 collective-permute-start.156
  23.2 4.4 %collective-permute-done.157 = bf16[128,1024]{1,0:T(8,128)(2,1)} collective-permute-done((bf16[128,1024]{1,0:T(8,128)(2,1)S(1)}, bf16[128,1024]{1,0:T(8,128)(2,1)}, u32[]{:S(2)}, u32[]{:S(2)}) %collective-permute-start.157) | collective-permute-done | bytes 262176 | tf_op jit(solution)/shard_map/cond/branch_22_fun/ppermute | solution.py:416
  27.6 0.0 collective-permute-start.158
  27.6 0.0 collective-permute-done.159
  27.6 0.5 %collective-permute-start.160 = (bf16[128,1024]{1,0:T(8,128)(2,1)}, bf16[128,1024]{1,0:T(8,128)(2,1)}, u32[]{:S(2)}, u32[]{:S(2)}) collective-permute-start(bf16[128,1024]{1,0:T(8,128)(2,1)} %collective-permute-done.159), channel_id=1, source_target_pairs={{1,0},{0,1},{3,2},{2,3},{5,4},{4,5},{7,6},{6,7},{9,8},{8,9},{11,10... | collective-permute-start | bytes 786440 | tf_op jit(solution)/shard_map/cond/branch_22_fun/ppermute | solution.py:422
  28.1 0.0 collective-permute-done.154
  28.1 0.0 collective-permute-done.156
  28.1 1.4 %collective-permute-done.158 = bf16[128,1024]{1,0:T(8,128)(2,1)} collective-permute-done((bf16[128,1024]{1,0:T(8,128)(2,1)}, bf16[128,1024]{1,0:T(8,128)(2,1)}, u32[]{:S(2)}, u32[]{:S(2)}) %collective-permute-start.158) | collective-permute-done | bytes 262176 | tf_op jit(solution)/shard_map/cond/branch_22_fun/ppermute | solution.py:422
  29.5 0.4 collective-permute-done.160
  29.9 0.0 copy-done.4
  29.9 6.0 %lags_to_send.1 = bf16[4,3,128,128]{3,2,1,0:T(8,128)(2,1)S(1)} custom-call(s32[2,4]{1,0:T(2,128)S(1)} %bitcast.3, s32[4]{0:T(128)S(1)} %copy-done.1, s32[128]{0:T(128)S(1)} %copy-done.2, f32[2,8,512]{2,1,0:T(8,128)S(1)} %copy-done.4, bf16[2,16,512]{2,1,0:T(8,128)(2,1)S(1)} %copy-done.3, bf16[128,1024]{1,0:T(8,128)(2,1)S(1)} %get-tuple-element.305.refs_0_, ...), custom_call_target="tpu_custom_call" | custom-call | flops 805306368 | bytes 2097152 | tf_op jit(solution)/shard_map/lags_to_send/pallas_call | solution.py:445
  35.9 0.6 %collective-permute-start.168 = (bf16[4,3,128,128]{3,2,1,0:T(8,128)(2,1)S(1)}, bf16[4,3,128,128]{3,2,1,0:T(8,128)(2,1)S(1)}, u32[]{:S(2)}, u32[]{:S(2)}) collective-permute-start(bf16[4,3,128,128]{3,2,1,0:T(8,128)(2,1)S(1)} %lags_to_send.1), channel_id=1, source_target_pairs={{0,2},{2,0},{1,3},{3,1},{4,6},{6,4},{5,7},{7,5},{8,10},{10,8},{9,1... | collective-permute-start | bytes 1179656 | tf_op jit(solution)/shard_map/ppermute | solution.py:471
  36.5 6.0 %lags_to_keep.1 = f32[4,3,128,128]{3,2,1,0:T(8,128)S(1)} custom-call(s32[2,4]{1,0:T(2,128)S(1)} %bitcast.4, s32[4]{0:T(128)S(1)} %copy-done.1, s32[128]{0:T(128)S(1)} %copy-done.2, f32[2,8,512]{2,1,0:T(8,128)S(1)} %copy-done.4, bf16[2,16,512]{2,1,0:T(8,128)(2,1)S(1)} %copy-done.3, bf16[128,1024]{1,0:T(8,128)(2,1)S(1)} %get-tuple-element.305.refs_0_, ...), custom_call_target="tpu_custom_call" | custom-call | flops 805306368 | bytes 2097152 | tf_op jit(solution)/shard_map/lags_to_keep/pallas_call | solution.py:445
  42.6 4.6 %collective-permute-done.168 = bf16[4,3,128,128]{3,2,1,0:T(8,128)(2,1)S(1)} collective-permute-done((bf16[4,3,128,128]{3,2,1,0:T(8,128)(2,1)S(1)}, bf16[4,3,128,128]{3,2,1,0:T(8,128)(2,1)S(1)}, u32[]{:S(2)}, u32[]{:S(2)}) %collective-permute-start.168) | collective-permute-done | bytes 393248 | tf_op jit(solution)/shard_map/ppermute | solution.py:471
  47.2 0.9 %multiply_convert_fusion = bf16[4,3,128,128]{3,2,1,0:T(8,128)(2,1)} fusion(f32[4,3,128,128]{3,2,1,0:T(8,128)S(1)} %lags_to_keep.1, bf16[4,3,128,128]{3,2,1,0:T(8,128)(2,1)S(1)} %collective-permute-done.168), kind=kLoop, calls=%fused_computation | loop fusion | flops 786432 | bytes 1572864 | tf_op jit(solution)/shard_map/convert_element_type | solution.py:475
  (7 shorter events, 0.0 us)
Async XLA Ops:
  0.0 29.9 %copy-start.2 = (s32[128]{0:T(128)S(1)}, s32[128]{0:T(128)}, u32[]{:S(2)}) copy-start(s32[128]{0:T(128)} %constant.14.clone.case_hbm.case_ref) | copy-start | bytes 1540
  0.0 29.9 %copy-start.3 = (bf16[2,16,512]{2,1,0:T(8,128)(2,1)S(1)}, bf16[2,16,512]{2,1,0:T(8,128)(2,1)}, u32[]{:S(2)}) copy-start(bf16[2,16,512]{2,1,0:T(8,128)(2,1)} %constant.16.clone.offset_ref) | copy-start | bytes 98308
  0.0 29.9 %copy-start.4 = (f32[2,8,512]{2,1,0:T(8,128)S(1)}, f32[2,8,512]{2,1,0:T(8,128)}, u32[]{:S(2)}) copy-start(f32[2,8,512]{2,1,0:T(8,128)} %constant.15.clone.turn_ref) | copy-start | bytes 98308
  0.0 29.9 %copy-start.1 = (s32[4]{0:T(128)S(1)}, s32[4]{0:T(128)}, u32[]{:S(2)}) copy-start(s32[4]{0:T(128)} %owner_ref.3) | copy-start | bytes 52
  0.0 29.9 %copy-start = (s32[4,2]{0,1:T(2,128)S(1)}, s32[4,2]{0,1:T(2,128)}, u32[]{:S(2)}) copy-start(s32[4,2]{0,1:T(2,128)} %param.32) | copy-start | bytes 100
  5.4 17.8 %collective-permute-start.155 = (bf16[128,1024]{1,0:T(8,128)(2,1)S(1)}, bf16[128,1024]{1,0:T(8,128)(2,1)}, u32[]{:S(2)}, u32[]{:S(2)}) collective-permute-start(bf16[128,1024]{1,0:T(8,128)(2,1)S(1)} %get-tuple-element.286), channel_id=1, source_target_pairs={{4,12},{5,13},{6,14},{7,15},{20,28},{21,29},{22,30},{23,31}} | collective-permute-start | bytes 786440 | tf_op jit(solution)/shard_map/cond/branch_22_fun/ppermute | solution.py:416
  6.7 20.9 %collective-permute-start.157 = (bf16[128,1024]{1,0:T(8,128)(2,1)S(1)}, bf16[128,1024]{1,0:T(8,128)(2,1)}, u32[]{:S(2)}, u32[]{:S(2)}) collective-permute-start(bf16[128,1024]{1,0:T(8,128)(2,1)S(1)} %get-tuple-element.287), channel_id=1, source_target_pairs={{8,12},{4,8},{9,13},{5,9},{10,14},{6,10},{11,15},{7,11},{24,28},{2... | collective-permute-start | bytes 786440 | tf_op jit(solution)/shard_map/cond/branch_22_fun/ppermute | solution.py:416
  8.0 19.6 %collective-permute-start.159 = (bf16[128,1024]{1,0:T(8,128)(2,1)S(1)}, bf16[128,1024]{1,0:T(8,128)(2,1)}, u32[]{:S(2)}, u32[]{:S(2)}) collective-permute-start(bf16[128,1024]{1,0:T(8,128)(2,1)S(1)} %get-tuple-element.288), channel_id=1, source_target_pairs={{0,12},{12,8},{1,13},{13,9},{2,14},{14,10},{3,15},{15,11},{16,28},... | collective-permute-start | bytes 786440 | tf_op jit(solution)/shard_map/cond/branch_22_fun/ppermute | solution.py:416
  12.6 15.5 %collective-permute-start.154 = (bf16[128,1024]{1,0:T(8,128)(2,1)S(1)}, bf16[128,1024]{1,0:T(8,128)(2,1)}, u32[]{:S(2)}, u32[]{:S(2)}) collective-permute-start(bf16[128,1024]{1,0:T(8,128)(2,1)S(1)} %get-tuple-element.285), channel_id=1, source_target_pairs={{1,0},{0,1},{3,2},{2,3},{5,4},{4,5},{7,6},{6,7},{9,8},{8,9},{11,10... | collective-permute-start | bytes 786440 | tf_op jit(solution)/shard_map/cond/branch_22_fun/ppermute | solution.py:422
  23.2 4.9 %collective-permute-start.156 = (bf16[128,1024]{1,0:T(8,128)(2,1)}, bf16[128,1024]{1,0:T(8,128)(2,1)}, u32[]{:S(2)}, u32[]{:S(2)}) collective-permute-start(bf16[128,1024]{1,0:T(8,128)(2,1)} %collective-permute-done.155), channel_id=1, source_target_pairs={{1,0},{0,1},{3,2},{2,3},{5,4},{4,5},{7,6},{6,7},{9,8},{8,9},{11,10... | collective-permute-start | bytes 786440 | tf_op jit(solution)/shard_map/cond/branch_22_fun/ppermute | solution.py:422
  27.6 1.9 %collective-permute-start.158 = (bf16[128,1024]{1,0:T(8,128)(2,1)}, bf16[128,1024]{1,0:T(8,128)(2,1)}, u32[]{:S(2)}, u32[]{:S(2)}) collective-permute-start(bf16[128,1024]{1,0:T(8,128)(2,1)} %collective-permute-done.157), channel_id=1, source_target_pairs={{1,0},{0,1},{3,2},{2,3},{5,4},{4,5},{7,6},{6,7},{9,8},{8,9},{11,10... | collective-permute-start | bytes 786440 | tf_op jit(solution)/shard_map/cond/branch_22_fun/ppermute | solution.py:422
  27.6 2.2 %collective-permute-start.160 = (bf16[128,1024]{1,0:T(8,128)(2,1)}, bf16[128,1024]{1,0:T(8,128)(2,1)}, u32[]{:S(2)}, u32[]{:S(2)}) collective-permute-start(bf16[128,1024]{1,0:T(8,128)(2,1)} %collective-permute-done.159), channel_id=1, source_target_pairs={{1,0},{0,1},{3,2},{2,3},{5,4},{4,5},{7,6},{6,7},{9,8},{8,9},{11,10... | collective-permute-start | bytes 786440 | tf_op jit(solution)/shard_map/cond/branch_22_fun/ppermute | solution.py:422
  35.9 11.2 %collective-permute-start.168 = (bf16[4,3,128,128]{3,2,1,0:T(8,128)(2,1)S(1)}, bf16[4,3,128,128]{3,2,1,0:T(8,128)(2,1)S(1)}, u32[]{:S(2)}, u32[]{:S(2)}) collective-permute-start(bf16[4,3,128,128]{3,2,1,0:T(8,128)(2,1)S(1)} %lags_to_send.1), channel_id=1, source_target_pairs={{0,2},{2,0},{1,3},{3,1},{4,6},{6,4},{5,7},{7,5},{8,10},{10,8},{9,1... | collective-permute-start | bytes 1179656 | tf_op jit(solution)/shard_map/ppermute | solution.py:471
